TPU v7x, 256 devices: a whole 4x4x8 slice. The times are simulated.
256 devices in a mesh: seq: 8 (over x, z_hi), cand: 32 (over z_lo, y, core).
Axes of the slice: x: 4, y: 4, z: 8 (z_hi: 2, z_lo: 4; z = z_hi * 4 + z_lo), core: 2. Of those that a mesh axis runs over, the one named last changes fastest.
Arguments:
- hist_x: bfloat16 [32, 1024, 1024], P('cand', 'seq'), may hold values from -6 to 6
- hist_len: int32 [32], replicated, may hold values from 1 to 1024, 20480 in all
- cand_x: bfloat16 [16384, 1024], P('cand'), may hold values from -6 to 6
- cand_user: int32 [16384, 1], P('cand'), may hold values from 0 to 31; in each aligned block of 512 rows (0 to 511, 512 to 1023, ...) at most 32 rows name the same one
- w_proj: bfloat16 [1024, 4096], replicated, may hold values from -0.1875 to 0.1875
- w_out: bfloat16 [1024, 1024], replicated, may hold values from -0.1875 to 0.1875
- norm_gain: float32 [1024], replicated, may hold values from 0.1 to 1.9
Outputs:
- hist_out: bfloat16 [32, 1024, 1024], P('cand', 'seq')
- cand_out: bfloat16 [16384, 1024], P('cand')
Inputs may be any that keep to these rules, and one draw needn't show every extreme that they name: `cand_user`: of the 512 rows on one index of cand, at most 32 belong to one user. `hist_len`: the longest history has exactly 1024 events.
All inputs are finite; a program needn't handle non-finite values.
Results may differ from a plain program's by a relative error of at most 0.011.
Values may be sent and summed in bfloat16 or wider, within the bound.
A program may use at most 128 MiB of HBM per device.

v0:
```python
import jax
import jax.numpy as jnp
from jax import lax
from jax.sharding import PartitionSpec as P

HEADS = 8


KEY_BLOCK = 512


def attend_block(queries, query_pos, keys_in, values_in, key_start, length, causal):
    query_count = queries.shape[0]
    key_count = keys_in.shape[0]
    model_width = queries.shape[1]
    per_head = model_width // HEADS
    needed = key_start < length
    if causal:
        needed = needed & (key_start <= query_pos[query_count - 1])

    def compute():
        query_heads = queries.reshape(query_count, HEADS, per_head)
        key_heads = keys_in.reshape(key_count, HEADS, per_head)
        value_heads = values_in.reshape(key_count, HEADS, per_head)
        scores = jnp.einsum(
            "qhe,khe->hqk", query_heads, key_heads, preferred_element_type=jnp.float32
        ) * per_head ** (-0.5)
        key_pos = key_start + jnp.arange(key_count, dtype=jnp.int32)
        allowed = key_pos[None, :] < length
        if causal:
            allowed = allowed & (key_pos[None, :] <= query_pos[:, None])
        weights = jnp.where(allowed[None], jax.nn.silu(scores), 0.0).astype(jnp.bfloat16)
        mixed_out = jnp.einsum(
            "hqk,khe->qhe", weights, value_heads, preferred_element_type=jnp.float32
        )
        return mixed_out.reshape(query_count, model_width)

    def nothing():
        return jnp.zeros((query_count, model_width), jnp.float32)

    return lax.cond(needed, compute, nothing)


def attend(queries, query_pos, keys_in, values_in, key_start, length, causal):
    key_count = keys_in.shape[0]
    if key_count > KEY_BLOCK and key_count % KEY_BLOCK == 0:
        blocks = key_count // KEY_BLOCK
        key_blocks = keys_in.reshape(blocks, KEY_BLOCK, keys_in.shape[1])
        value_blocks = values_in.reshape(blocks, KEY_BLOCK, values_in.shape[1])

        def step_block(carried, packed):
            block_id, key_part, value_part = packed
            added = attend_block(
                queries, query_pos, key_part, value_part, block_id * KEY_BLOCK, length, causal
            )
            return (carried + added, None)

        initial = jnp.zeros(queries.shape, jnp.float32)
        summed, ignored = lax.scan(
            step_block, initial, (jnp.arange(blocks, dtype=jnp.int32), key_blocks, value_blocks)
        )
        return summed
    return attend_block(queries, query_pos, keys_in, values_in, key_start, length, causal)


def finish_rows(totals, norm_gain, gate_rows, inputs, w_out):
    average = jnp.mean(totals, axis=-1, keepdims=True)
    centred = totals - average
    variance = jnp.mean(centred * centred, axis=-1, keepdims=True)
    normed = (
        centred * lax.rsqrt(variance + 1e-05) * norm_gain * gate_rows.astype(jnp.float32)
    ).astype(jnp.bfloat16)
    result = jnp.dot(normed, w_out, preferred_element_type=jnp.float32) + inputs.astype(jnp.float32)
    return result.astype(jnp.bfloat16)


def finish_whole(totals, cand_x, w_proj, norm_gain, w_out):
    model_width = cand_x.shape[1]
    gate_cand = jax.nn.silu(
        jnp.dot(cand_x, w_proj[:, :model_width], preferred_element_type=jnp.float32)
    ).astype(jnp.bfloat16)
    return finish_rows(totals, norm_gain, gate_cand, cand_x, w_out)


def per_device(hist_x, hist_len, cand_x, cand_user, w_proj, w_out, norm_gain):
    history = hist_x[0]
    local_len = history.shape[0]
    model_width = history.shape[1]
    seq_index = lax.axis_index("seq")
    user_index = lax.axis_index("cand")
    length = hist_len[user_index]
    projected = jax.nn.silu(jnp.dot(history, w_proj, preferred_element_type=jnp.float32)).astype(
        jnp.bfloat16
    )
    gate_hist = projected[:, :model_width]
    value_hist = projected[:, model_width : 2 * model_width]
    query_hist = projected[:, 2 * model_width : 3 * model_width]
    key_hist = projected[:, 3 * model_width :]
    first_row = seq_index * local_len
    query_pos = first_row + jnp.arange(local_len, dtype=jnp.int32)
    encoded = attend(
        query_hist,
        query_pos,
        lax.all_gather(key_hist, "seq", axis=0, tiled=True),
        lax.all_gather(value_hist, "seq", axis=0, tiled=True),
        jnp.int32(0),
        length,
        True,
    )
    hist_out = finish_rows(encoded, norm_gain, gate_hist, history, w_out)[None]
    cand_rows = cand_x.shape[0]
    groups = lax.axis_size("cand")
    capacity = 2 * cand_rows // groups
    query_cand = jax.nn.silu(
        jnp.dot(
            cand_x, w_proj[:, 2 * model_width : 3 * model_width], preferred_element_type=jnp.float32
        )
    ).astype(jnp.bfloat16)
    owners = cand_user[:, 0]
    onehot = (owners[:, None] == jnp.arange(groups, dtype=jnp.int32)[None, :]).astype(jnp.int32)
    earlier = jnp.cumsum(onehot, axis=0) - onehot
    within = jnp.sum(earlier * onehot, axis=1)
    target = owners * capacity + within
    selector = (jnp.arange(groups * capacity, dtype=jnp.int32)[:, None] == target[None, :]).astype(
        jnp.bfloat16
    )
    outgoing = jnp.dot(selector, query_cand, preferred_element_type=jnp.float32).astype(
        jnp.bfloat16
    )
    outgoing = outgoing.reshape(groups, capacity, model_width)
    arrived = lax.all_to_all(outgoing, "cand", split_axis=0, concat_axis=0, tiled=True)
    flattened = arrived.reshape(-1, model_width)
    partial_value = attend(flattened, None, key_hist, value_hist, first_row, length, False).reshape(
        arrived.shape
    )
    returned = lax.all_to_all(partial_value, "cand", split_axis=0, concat_axis=0, tiled=True)
    gathered = jnp.take(returned.reshape(groups * capacity, model_width), target, axis=0)
    totals = lax.psum(gathered, "seq")
    cand_out = finish_whole(totals, cand_x, w_proj, norm_gain, w_out)
    return (hist_out, cand_out)


def solution(mesh):
    in_specs = (P("cand", "seq", None), P(), P("cand", None), P("cand", None), P(), P(), P())
    out_specs = (P("cand", "seq", None), P("cand", None))
    return jax.shard_map(
        per_device, mesh=mesh, in_specs=in_specs, out_specs=out_specs, check_vma=False
    )
```

profile of v0, /device:TPU:1, one launch (start us, length us, event | category | flops | bytes accessed | tf_op | source)
XLA Modules:
  0.0 484.6 jit_solution(14485913301219076604)
XLA Ops:
  7.2 0.8 fusion.61
  8.0 1.2 reduce-window.6
  9.4 0.8 fusion.60
  10.2 0.7 multiply_add_fusion
  10.9 5.8 %fusion.33 = bf16[1024,1024]{1,0:T(8,128)(2,1)} fusion(s32[512]{0:T(512)S(1)} %multiply_add_fusion, bf16[512,1024]{1,0:T(8,128)(2,1)} %param.15, bf16[1024,4096]{1,0:T(8,128)(2,1)} %param.17), kind=kOutput, calls=%fused_computation.45 | convolution fusion | flops 2151677952 | bytes 5244928 | tf_op jit(solution)/shard_map/dot_general | solution.py:127
  16.7 10.4 %all-to-all-start = ((bf16[32,32,1024]{2,1,0:T(8,128)(2,1)}), bf16[32,32,1024]{2,1,0:T(8,128)(2,1)}, u32[]{:S(2)}, u32[]{:S(2)}) async-start(bf16[32,32,1024]{2,1,0:T(8,128)(2,1)} %bitcast.105), calls=%async_computation | async-start | bytes 4194304 | tf_op jit(solution)/shard_map/all_to_all | solution.py:131
  28.4 4.7 multiply_convert_fusion.3
  33.1 1.0 copy-done.2
  34.1 0.8 fusion.64
  34.8 40.5 %all-to-all-done = bf16[32,32,1024]{2,1,0:T(8,128)(2,1)} async-done(((bf16[32,32,1024]{2,1,0:T(8,128)(2,1)}), bf16[32,32,1024]{2,1,0:T(8,128)(2,1)}, u32[]{:S(2)}, u32[]{:S(2)}) %all-to-all-start) | async-done | bytes 2097184 | tf_op jit(solution)/shard_map/all_to_all | solution.py:131
  75.3 9.8 %conditional.2 = (f32[1024,1024]{0,1:T(8,128)}) conditional(s32[]{:T(128)} %convert_element_type.65, () %tuple.29, (s32[]{:T(128)}, s32[]{:T(128)}, bf16[32,32,1024]{2,1,0:T(8,128)(2,1)}, bf16[128,1024]{1,0:T(8,128)(2,1)S(1)}, bf16[128,1024]{1,0:T(8,128)(2,1)S(1)}) %tuple.30), branch_computations={%region_9.10_spmd, %region_10.11_spmd} | conditional | flops 544211200 | bytes 11534608 | solution.py:41
  75.5 3.6 copy.32
  79.7 5.5 %fusion.19 = f32[8,1024,128]{1,2,0:T(8,128)} fusion(bf16[128,8,128]{0,2,1:T(8,128)(2,1)S(1)} %bitcast.107, bf16[1024,8,128]{2,1,0:T(8,128)(2,1)} %bitcast.106, pred[128]{0:T(512)(128)(4,1)S(1)} %add_compare_fusion, bf16[128,1024]{1,0:T(8,128)(2,1)S(1)} %get-tuple-element.120), kind=kOutput, calls=%fused_computation.25 | convolution fusion | flops 544210944 | bytes 6815872 | tf_op jit(solution)/shard_map/cond/branch_1_fun/hqk,khe->qhe/dot_general | solution.py:33
  85.1 5.3 %copy.27 = f32[1024,1024]{1,0:T(8,128)} copy(f32[1024,1024]{0,1:T(8,128)} %get-tuple-element.284) | data formatting | bytes 8388608 | tf_op jit(solution)/shard_map/cond | solution.py:41
  90.5 6.5 %all-to-all-start.1 = ((f32[32,32,1024]{2,1,0:T(8,128)}), f32[32,32,1024]{2,1,0:T(8,128)}, u32[]{:S(2)}, u32[]{:S(2)}) async-start(f32[32,32,1024]{2,1,0:T(8,128)} %bitcast.101), calls=%async_computation.1 | async-start | bytes 8388608 | tf_op jit(solution)/shard_map/all_to_all | solution.py:136
  97.1 0.7 all-gather.3.cloned.1.call-update
  97.8 0.7 all-gather.5.cloned.1.call-update
  98.8 125.3 %all-to-all-done.1 = f32[32,32,1024]{2,1,0:T(8,128)} async-done(((f32[32,32,1024]{2,1,0:T(8,128)}), f32[32,32,1024]{2,1,0:T(8,128)}, u32[]{:S(2)}, u32[]{:S(2)}) %all-to-all-start.1) | async-done | bytes 4194336 | tf_op jit(solution)/shard_map/all_to_all | solution.py:136
  224.1 5.8 %gather_fusion = f32[512,1024]{1,0:T(8,128)} fusion(f32[1024,1024]{1,0:T(8,128)} %bitcast.19, s32[1024]{0:T(1024)S(1)} %pad_clamp_fusion), kind=kCustom, calls=%fused_computation | custom fusion | bytes 4196352 | tf_op jit(solution)/shard_map/jit(_take)/gather | solution.py:137
  229.9 3.1 broadcast_select_fusion
  233.1 4.0 copy.22
  237.1 37.3 %all-gather.5.cloned.1.call-done = bf16[1024,1024]{1,0:T(8,128)(2,1)} async-done(((bf16[128,1024]{1,0:T(8,128)(2,1)}), bf16[1024,1024]{1,0:T(8,128)(2,1)}) %all-gather.5.cloned.1.call-update) | async-done | bytes 2097168 | tf_op jit(solution)/shard_map/all_gather | solution.py:105
  274.4 4.0 copy.23
  278.4 12.8 %while.11 = (s32[]{:T(128)}, f32[128,1024]{0,1:T(8,128)S(1)}, s32[2]{0:T(128)S(1)}, s32[]{:T(128)}, s32[128]{0:T(128)S(1)}, /*index=5*/bf16[2,512,1024]{1,2,0:T(...) while((s32[]{:T(128)}, f32[128,1024]{0,1:T(8,128)S(1)}, ...), condition=%wide.region_3.4_spmd.clone, body=%wide.region_0.3_spmd.clone.sunk | while | flops 272500224 | bytes 8787721 | solution.py:59
  281.2 6.7 %conditional.5 = (f32[128,1024]{0,1:T(8,128)S(1)}) conditional(s32[]{:T(128)} %convert_element_type.105, () %tuple.56, (s32[]{:T(128)}, s32[]{:T(128)}, s32[128]{0:T(128)S(1)}, bf16[2,512,1024]{1,2,0:T(8,128)(2,1)}, s32[]{:T(128)}, /*index=5*/bf16[128,1024]{1,0:T(8,128)(2,1)}, bf16[2,512,1024]{1,2,0:T(8,128)(2,1)}) %tuple.57), branch_computations={%region_1.1_spmd, %region_2.2_spmd} | conditional | flops 272238080 | bytes 7214616 | solution.py:41
  281.3 3.1 constant_dynamic-slice_fusion
  285.2 2.8 fusion.5
  291.9 2.2 fusion.35
  294.1 173.8 %all-reduce.2.cloned.1.call-done = f32[512,1024]{1,0:T(8,128)} async-done(((f32[512,1024]{1,0:T(8,128)}), f32[512,1024]{1,0:T(8,128)}) %all-reduce.2.cloned.1.call-update) | async-done | bytes 2097168 | tf_op jit(solution)/shard_map/psum | solution.py:138
  467.9 1.8 reduce_sum.51
  469.7 1.9 multiply_reduce_fusion
  471.6 6.4 %add_convert_fusion = bf16[512,1024]{1,0:T(8,128)(2,1)} fusion(bf16[512,1024]{1,0:T(8,128)(2,1)} %param.15, bf16[1024,1024]{1,0:T(8,128)(2,1)S(1)} %copy-done, f32[512,1024]{1,0:T(8,128)} %all-reduce.2.cloned.1.call-done, f32[1024]{0:T(1024)S(1)} %copy-done.6, f32[512]{0:T(512)S(1)} %add_rsqrt_fusion, f32[512]{0:T(512)S(1)} %broadcast_multiply_fusion, ...), kind=kOutput, calls=%fused_computation.33 | convolution fusion | flops 2154823680 | bytes 9445376 | tf_op jit(solution)/shard_map/dot_general | solution.py:73
  (49 shorter events, 6.2 us)
Async XLA Ops:
  7.2 284.6 %copy-start = (bf16[1024,1024]{1,0:T(8,128)(2,1)S(1)}, bf16[1024,1024]{1,0:T(8,128)(2,1)}, u32[]{:S(2)}) copy-start(bf16[1024,1024]{1,0:T(8,128)(2,1)} %param.18) | copy-start | bytes 6291460
  16.7 10.4 %copy-start.7 = (s32[32]{0:T(128)S(1)}, s32[32]{0:T(128)}, u32[]{:S(2)}) copy-start(s32[32]{0:T(128)} %param.14) | copy-start | bytes 388
  16.7 11.6 %copy-start.4 = (bf16[1,128,1024]{2,1,0:T(8,128)(2,1)S(1)}, bf16[1,128,1024]{2,1,0:T(8,128)(2,1)}, u32[]{:S(2)}) copy-start(bf16[1,128,1024]{2,1,0:T(8,128)(2,1)} %param.13) | copy-start | bytes 786436
  16.7 58.6 %all-to-all-start = ((bf16[32,32,1024]{2,1,0:T(8,128)(2,1)}), bf16[32,32,1024]{2,1,0:T(8,128)(2,1)}, u32[]{:S(2)}, u32[]{:S(2)}) async-start(bf16[32,32,1024]{2,1,0:T(8,128)(2,1)} %bitcast.105), calls=%async_computation | async-start | bytes 4194304 | tf_op jit(solution)/shard_map/all_to_all | solution.py:131
  33.1 1.0 copy-start.2
  34.8 40.5 %copy-start.1 = (bf16[128,1024]{1,0:T(8,128)(2,1)}, bf16[128,1024]{1,0:T(8,128)(2,1)S(1)}, u32[]{:S(2)}) copy-start(bf16[128,1024]{1,0:T(8,128)(2,1)S(1)} %get-tuple-element.199) | copy-start | bytes 786436
  34.8 40.5 %copy-start.3 = (bf16[128,1024]{1,0:T(8,128)(2,1)}, bf16[128,1024]{1,0:T(8,128)(2,1)S(1)}, u32[]{:S(2)}) copy-start(bf16[128,1024]{1,0:T(8,128)(2,1)S(1)} %get-tuple-element.201) | copy-start | bytes 786436
  90.5 8.3 %copy-start.5 = (s32[512,1]{0,1:T(1,128)S(1)}, s32[512,1]{0,1:T(1,128)}, u32[]{:S(2)}) copy-start(s32[512,1]{0,1:T(1,128)} %param.16) | copy-start | bytes 6148
  90.5 133.6 %all-to-all-start.1 = ((f32[32,32,1024]{2,1,0:T(8,128)}), f32[32,32,1024]{2,1,0:T(8,128)}, u32[]{:S(2)}, u32[]{:S(2)}) async-start(f32[32,32,1024]{2,1,0:T(8,128)} %bitcast.101), calls=%async_computation.1 | async-start | bytes 8388608 | tf_op jit(solution)/shard_map/all_to_all | solution.py:136
  97.0 136.1 %all-gather.3.cloned.1.call-start = ((), (), s32[]{:S(2)}) async-start(), calls=%async_computation.2 | async-start | bytes 2359296 | tf_op jit(solution)/shard_map/all_gather | solution.py:104
  97.8 176.6 %all-gather.5.cloned.1.call-start = ((), (), s32[]{:S(2)}) async-start(), calls=%async_computation.3 | async-start | bytes 2359296 | tf_op jit(solution)/shard_map/all_gather | solution.py:105
  98.5 369.4 %all-reduce.2.cloned.1.call-start = ((), (), s32[]{:S(2)}) async-start(), calls=%async_computation.4 | async-start | bytes 4194304 | tf_op jit(solution)/shard_map/psum | solution.py:138
  291.2 0.7 copy-start.6
Sparse Core Ops, SparseCore 0:
  100.5 96.4 all-gather.2
  199.6 74.7 all-gather.4
  277.1 190.7 all-reduce.1
where the time goes:
time: 484 us; the launch traced here: 485 us
  waiting for transfers between devices  378 us (78%)
  local copies, waits for them, and re-layouts  31.1 us (6%)
  matrix products  27.4 us (6%)
  starting transfers between devices  17.2 us (4%)
  between operations  14.5 us (3%)
  other arithmetic  12.5 us (3%)
    psum x1, waiting for transfers between devices, per_device(): totals = lax.psum(gathered, 'seq')  174 us
    all_to_all x1, waiting for transfers between devices, per_device(): lax.all_to_all(partial_value, 'cand', split_axis=0, concat_axis=0, tiled=...  125 us
    all_to_all x1, waiting for transfers between devices, per_device(): lax.all_to_all(outgoing, 'cand', split_axis=0, concat_axis=0, tiled=True)  40.5 us
    all_gather x1, waiting for transfers between devices, per_device(): lax.all_gather(value_hist, 'seq', axis=0, tiled=True)  37.3 us
    all_to_all x1, starting transfers between devices, per_device(): lax.all_to_all(outgoing, 'cand', split_axis=0, concat_axis=0, tiled=True)  10.4 us
  transfers between devices with their start and end apart: 5, of which 4 were waited for; matrix products, arithmetic and copies ran while one was open for 7% of the time, Pallas kernels for 0%

commit v1 on v0

v1 whole, which is shorter than its diff:
```python
import jax
import jax.numpy as jnp
from jax import lax
from jax.experimental import pallas as pl
from jax.experimental.pallas import tpu as pltpu
from jax.sharding import PartitionSpec as P


HEADS = 8
HEAD = 128
D = 1024
ROWS = 128
CHUNKS = 4
CROWS = ROWS // CHUNKS
CAND = 512
QUARTER = 256
MESH = pl.DeviceIdType.MESH
BF = jnp.bfloat16
F32 = jnp.float32
I32 = jnp.int32
NT = (((1,), (1,)), ((), ()))


def silu(a):
    half = 0.5 * a
    return half + half * jnp.tanh(half)


def iota(shape, dim):
    return lax.broadcasted_iota(I32, shape, dim)


def onehot(condition):
    return jnp.where(condition, 1.0, 0.0).astype(BF)


def dot(a, b):
    return jnp.dot(a, b, preferred_element_type=F32)


def remote(src, dst, send, recv, seq, cand):
    return pltpu.make_async_remote_copy(
        src_ref=src, dst_ref=dst, send_sem=send, recv_sem=recv,
        device_id={"seq": seq, "cand": cand}, device_id_type=MESH,
    )


def kernel(
    x_hbm, len_ref, candx_hbm, cuser_ref, wp_hbm, wo_hbm, gain_ref,
    hist_ref, cand_ref,
    wp, wo, candx, xb, keys, values, xq, qg, acc, msgs, rdisp, back, rret, crep, unsort, sorted_rows, hist_tmp,
    load_sem, swap_send, swap_recv, x_send, x_recv, fwd_send, d_send, d_recv, r_send, r_recv, g_send, g_recv, h_sem,
):
    s = lax.axis_index("seq")
    c = lax.axis_index("cand")
    x, zh = s // 2, s % 2
    core, y, zl = c % 2, (c // 2) % 4, c // 8
    z = zh * 4 + zl
    user = c - core + zh
    other_core = c + 1 - 2 * core
    early = core == zh
    late = core != zh
    swap_seq = 2 * x + core
    my_row = pl.multiple_of((core * 4 + x) * ROWS, ROWS)

    barrier = pltpu.get_barrier_semaphore()

    def greet(i, carry):
        pl.semaphore_signal(
            barrier, inc=1, device_id={"seq": 2 * x + (zh + i // 32) % 2, "cand": (c + i) % 32}, device_id_type=MESH
        )
        return carry

    lax.fori_loop(1, 64, greet, 0)
    for i in range(1, 4):
        pl.semaphore_signal(
            barrier, inc=1, device_id={"seq": 2 * ((x + i) % 4) + zh, "cand": c}, device_id_type=MESH
        )

    def load(src, dst, i):
        return pltpu.make_async_copy(src, dst, load_sem.at[i])

    own_load = load(x_hbm, xb.at[pl.ds(my_row, ROWS)], 0)
    cand_load = load(candx_hbm, candx, 1)
    wp_load = load(wp_hbm, wp, 2)
    wo_load = load(wo_hbm, wo, 3)

    @pl.when(early)
    def _():
        own_load.start()

    cand_load.start()
    wp_load.start()
    wo_load.start()

    @pl.when(early)
    def _():
        own_load.wait()

    pl.semaphore_wait(barrier, 66)

    def swap_copy(j):
        rows = pl.ds(pl.multiple_of((zh * 4 + x) * ROWS + j * CROWS, CROWS), CROWS)
        return remote(
            x_hbm.at[pl.ds(j * CROWS, CROWS)], xb.at[rows], swap_send.at[j], swap_recv.at[j], swap_seq, user
        )

    def own_rows(j):
        return xb.at[pl.ds(pl.multiple_of(my_row + j * CROWS, CROWS), CROWS)]

    def own_copy(i, j):
        recv = x_recv.at[(core * 4 + x) * CHUNKS + j]
        if i == 0:
            return remote(own_rows(j), own_rows(j), x_send.at[j], recv, s, other_core)
        return remote(own_rows(j), own_rows(j), x_send.at[i * CHUNKS + j], recv, 2 * ((x + i) % 4) + zh, c)

    def slot_rows(slot, j):
        return xb.at[pl.ds(pl.multiple_of(slot * ROWS + j * CROWS, CROWS), CROWS)]

    def slot_wait(slot, j):
        rows = slot_rows(slot, j)
        recv = x_recv.at[slot * CHUNKS + j]
        remote(rows, rows, fwd_send.at[0], recv, s, other_core).wait_recv()

    def fwd_copy(i, j):
        slot = core * 4 + (x + i) % 4
        rows = slot_rows(slot, j)
        return remote(rows, rows, fwd_send.at[(i - 1) * CHUNKS + j], x_recv.at[slot * CHUNKS + j], s, other_core)

    def forward():
        for j in range(CHUNKS):
            for i in range(1, 4):
                slot_wait(core * 4 + (x + i) % 4, j)
                fwd_copy(i, j).start()

    @pl.when(late)
    def _():
        for j in range(CHUNKS):
            swap_copy(j).start()

    @pl.when(early)
    def _():
        for j in range(CHUNKS):
            for i in range(4):
                own_copy(i, j).start()

    owner = cuser_ref[...]
    is_user = owner == iota((32, CAND), 0)
    users = onehot(is_user)
    before = dot(users, onehot(iota((CAND, CAND), 0) < iota((CAND, CAND), 1)))
    within = jnp.sum(jnp.where(is_user, before, 0.0), axis=0, keepdims=True).astype(I32)
    smaller = dot(onehot(iota((32, 32), 1) < iota((32, 32), 0)), users)
    start = jnp.sum(smaller, axis=1, keepdims=True)
    place = jnp.sum(jnp.where(is_user, start, 0.0), axis=0, keepdims=True).astype(I32) + within
    part = place & 7
    code = owner * 32 + part * 4 + (within >> 3)
    sorted_at = ((part >> 1) << 7) + ((part & 1) << 6) + (place >> 3)

    def message(m):
        which, dy = m >> 2, m & 3
        pair = which >> 1
        dz = jnp.where(
            pair == 0, 0, jnp.where(pair == 1, 1, jnp.where(pair == 2, 7, jnp.where(which == 6, 2, 6)))
        )
        dcore = which & 1
        tz = (z + dz) & 7
        ty = (y + dy) & 3
        tcore = (core + dcore) & 1
        column = (tz & 3) * 4 + ty
        return column * 2 + (tz >> 2), tz >> 2, column * 2 + tcore, tcore

    slot = iota((CAND, 1), 0)
    to_user, _, _, to_core = message(slot >> 4)
    slot_code = to_user * 32 + (2 * x + to_core) * 4 + (slot & 3)
    match = slot_code == code
    slot_quarter = (slot >> 2) & 3
    cand_load.wait()
    sent = jnp.zeros((CAND, QUARTER), F32)
    for j in range(4):
        sent += dot(onehot(match & (slot_quarter == j)), candx[:, j * QUARTER : (j + 1) * QUARTER])
    msgs[...] = sent.astype(BF)

    def piece(ref, i):
        return ref.at[pl.ds(pl.multiple_of(i * 16, 16), 16)]

    def d_copy(m):
        _, tzh, tcand, _ = message(m)
        return remote(piece(msgs, m), piece(rdisp, c), d_send.at[m], d_recv.at[c], 2 * x + tzh, tcand)

    self_d = pltpu.make_async_copy(piece(msgs, 0), piece(rdisp, c), d_recv.at[c])
    self_d.start()

    def send_d(m, carry):
        d_copy(m).start()
        return carry

    lax.fori_loop(1, 32, send_d, 0)

    ret = iota((1024, 1), 0)
    ret_to = ret >> 4
    ret_code = (ret_to >> 1) * 32 + (2 * x + (ret_to & 1)) * 4 + (ret & 3)
    mine = iota((ROWS, 1), 0)
    mine_place = 8 * (mine & 63) + 2 * x + (mine >> 6)
    crep[...] = lax.dot_general(
        onehot(mine_place == place), onehot(ret_code == code), NT, preferred_element_type=F32
    ).astype(BF)
    unsort[...] = lax.dot_general(
        onehot(iota((CAND, CAND), 0) == iota((CAND, CAND), 1)),
        onehot(iota((CAND, 1), 0) == sorted_at), NT, preferred_element_type=F32,
    ).astype(BF)

    @pl.when(late)
    def _():
        for j in range(CHUNKS):
            swap_copy(j).wait_recv()
            for i in range(4):
                own_copy(i, j).start()

    @pl.when(early)
    def _():
        forward()

    length = len_ref[user]

    def block_pos(kind, width_iota):
        return (2 * (width_iota >> 7) + kind) * ROWS + (width_iota & (ROWS - 1))

    def project(kind):
        top = pl.multiple_of(kind * 4 * ROWS, ROWS)
        rows = pl.ds(top, 4 * ROWS)
        alive = block_pos(kind, iota((4 * ROWS, 1), 0)) < length

        def step(n, carry):
            cols = pl.ds(pl.multiple_of(n * QUARTER, QUARTER), QUARTER)
            kcols = pl.ds(pl.multiple_of(3 * D + n * QUARTER, QUARTER), QUARTER)
            vcols = pl.ds(pl.multiple_of(D + n * QUARTER, QUARTER), QUARTER)
            keys[rows, cols] = silu(dot(xb[rows, :], wp[:, kcols])).astype(BF)
            values[rows, cols] = jnp.where(alive, silu(dot(xb[rows, :], wp[:, vcols])), 0.0).astype(BF)
            return carry

        lax.fori_loop(0, 4, step, 0)

    query_row = iota((2 * ROWS, 1), 0)
    query_pos = jnp.where(query_row < ROWS, (2 * x + core) * ROWS + query_row, 1 << 20)

    def attend(kind, first):
        top = pl.multiple_of(kind * 4 * ROWS, ROWS)
        rows = pl.ds(top, 4 * ROWS)
        allowed = block_pos(kind, iota((1, 4 * ROWS), 1)) <= query_pos

        def step(h, carry):
            cols = pl.ds(pl.multiple_of(h * HEAD, HEAD), HEAD)
            scores = lax.dot_general(qg[:, pl.ds(pl.multiple_of(D + h * HEAD, HEAD), HEAD)], keys[rows, cols], NT,
                                     preferred_element_type=F32)
            weights = jnp.where(allowed, silu(scores * HEAD ** -0.5), 0.0).astype(BF)
            mixed = dot(weights, values[rows, cols])
            if first:
                acc[:, cols] = mixed
            else:
                acc[:, cols] += mixed
            return carry

        lax.fori_loop(0, HEADS, step, 0)

    wp_load.wait()

    @pl.when(late)
    def _():
        for j in range(CHUNKS):
            for i in range(4):
                slot_wait((1 - core) * 4 + (x + i) % 4, j)

    project(zh)

    def wait_d(i, carry):
        there = (c + i) % 32
        remote(piece(rdisp, there), piece(rdisp, there), d_send.at[0], d_recv.at[there], s, other_core).wait_recv()
        return carry

    self_d.wait()
    lax.fori_loop(1, 32, wait_d, 0)
    here = iota((ROWS, CAND), 0)
    lane = iota((ROWS, CAND), 1)
    same = ((here >> 2) == (lane >> 4)) & ((here & 3) == (lane & 3))
    lane_quarter = (lane >> 2) & 3
    for j in range(4):
        xq[ROWS : 2 * ROWS, j * QUARTER : (j + 1) * QUARTER] = dot(
            onehot(same & (lane_quarter == j)), rdisp[...]
        ).astype(BF)
    xq[0:ROWS, :] = xb[pl.ds(my_row, ROWS), :]

    def project_q(n, carry):
        cols = pl.ds(pl.multiple_of(n * QUARTER, QUARTER), QUARTER)
        qcols = pl.ds(pl.multiple_of(D + n * QUARTER, QUARTER), QUARTER)
        wcols = pl.ds(pl.multiple_of(2 * D + n * QUARTER, QUARTER), QUARTER)
        qg[:, cols] = silu(dot(xq[...], wp[:, cols])).astype(BF)
        qg[:, qcols] = silu(dot(xq[...], wp[:, wcols])).astype(BF)
        return carry

    lax.fori_loop(0, 4, project_q, 0)
    attend(zh, True)

    @pl.when(late)
    def _():
        forward()

    @pl.when(early)
    def _():
        for j in range(CHUNKS):
            for i in range(4):
                slot_wait((1 - core) * 4 + (x + i) % 4, j)

    project(1 - zh)
    attend(1 - zh, False)

    wo_load.wait()

    def finish(first):
        rows = slice(first, first + ROWS)
        totals = acc[rows, :]
        average = jnp.mean(totals, axis=1, keepdims=True)
        centred = totals - average
        variance = jnp.mean(centred * centred, axis=1, keepdims=True)
        normed = (
            centred * lax.rsqrt(variance + 1e-05) * gain_ref[...] * qg[rows, 0:D].astype(F32)
        ).astype(BF)
        return (dot(normed, wo[...]) + xq[rows, :].astype(F32)).astype(BF)

    done = finish(ROWS)
    tall = iota((CAND, ROWS), 0)
    wide = iota((CAND, ROWS), 1)
    same_t = ((wide >> 2) == (tall >> 4)) & ((wide & 3) == (tall & 3))
    tall_quarter = (tall >> 2) & 3
    returned = jnp.zeros((CAND, QUARTER), F32)
    for j in range(4):
        returned += dot(onehot(same_t & (tall_quarter == j)), done[:, j * QUARTER : (j + 1) * QUARTER])
    back[...] = returned.astype(BF)
    my_ret = user * 2 + core

    def r_copy(i):
        there = (c + i) % 32
        return remote(
            piece(back, there), piece(rret, my_ret), r_send.at[i], r_recv.at[my_ret], 2 * x + (zh + i // 32) % 2, there
        )

    self_r = pltpu.make_async_copy(piece(back, c), piece(rret, my_ret), r_recv.at[my_ret])
    self_r.start()

    def send_r(i, carry):
        r_copy(i).start()
        return carry

    lax.fori_loop(1, 64, send_r, 0)

    done_hist = finish(0)
    hist_copy = remote(hist_tmp, hist_ref, h_sem.at[0], h_sem.at[1], swap_seq, user)

    @pl.when(early)
    def _():
        hist_ref[...] = done_hist

    @pl.when(late)
    def _():
        hist_tmp[...] = done_hist
        hist_copy.start()

    def wait_r(i, carry):
        there = (my_ret + i) % 64
        remote(piece(rret, there), piece(rret, there), d_send.at[0], r_recv.at[there], s, other_core).wait_recv()
        return carry

    self_r.wait()
    lax.fori_loop(1, 64, wait_r, 0)
    mine_rows = pl.ds(pl.multiple_of(x * ROWS, ROWS), ROWS)
    ret_quarter = (iota((ROWS, 1024), 1) >> 2) & 3
    for j in range(4):
        picked = jnp.where(ret_quarter == j, crep[...], jnp.zeros((), BF))
        sorted_rows[mine_rows, j * QUARTER : (j + 1) * QUARTER] = dot(picked, rret[...]).astype(BF)

    def g_copy(i):
        return remote(
            sorted_rows.at[mine_rows], sorted_rows.at[mine_rows], g_send.at[i], g_recv.at[x], 2 * ((x + i) % 4) + zh, c
        )

    for i in range(1, 4):
        g_copy(i).start()
    for i in range(1, 4):
        from_x = (x + i) % 4
        rows = sorted_rows.at[pl.ds(pl.multiple_of(from_x * ROWS, ROWS), ROWS)]
        remote(rows, rows, g_send.at[0], g_recv.at[from_x], s, other_core).wait_recv()

    def last(n, carry):
        cols = pl.ds(pl.multiple_of(n * QUARTER, QUARTER), QUARTER)
        cand_ref[:, cols] = dot(unsort[...], sorted_rows[:, cols]).astype(BF)
        return carry

    lax.fori_loop(0, 4, last, 0)

    for i in range(1, 4):
        g_copy(i).wait_send()

    def sent_r(i, carry):
        r_copy(i).wait_send()
        return carry

    lax.fori_loop(1, 64, sent_r, 0)

    def sent_d(m, carry):
        d_copy(m).wait_send()
        return carry

    lax.fori_loop(1, 32, sent_d, 0)
    for j in range(CHUNKS):
        for i in range(4):
            own_copy(i, j).wait_send()
        for i in range(1, 4):
            fwd_copy(i, j).wait_send()

    @pl.when(late)
    def _():
        for j in range(CHUNKS):
            swap_copy(j).wait_send()
        hist_copy.wait()


def per_device(hist_x, hist_len, cand_x, cand_user, w_proj, w_out, norm_gain):
    any_spec = pl.BlockSpec(memory_space=pl.ANY)
    vmem = pl.BlockSpec(memory_space=pltpu.VMEM)
    dma = pltpu.SemaphoreType.DMA
    hist_out, cand_out = pl.pallas_call(
        kernel,
        out_shape=(jax.ShapeDtypeStruct((ROWS, D), BF), jax.ShapeDtypeStruct((CAND, D), BF)),
        in_specs=[any_spec, pl.BlockSpec(memory_space=pltpu.SMEM), any_spec, vmem, any_spec, any_spec, vmem],
        out_specs=(vmem, vmem),
        scratch_shapes=[
            pltpu.VMEM((D, 4 * D), BF),
            pltpu.VMEM((D, D), BF),
            pltpu.VMEM((CAND, D), BF),
            pltpu.VMEM((8 * ROWS, D), BF),
            pltpu.VMEM((8 * ROWS, D), BF),
            pltpu.VMEM((8 * ROWS, D), BF),
            pltpu.VMEM((2 * ROWS, D), BF),
            pltpu.VMEM((2 * ROWS, 2 * D), BF),
            pltpu.VMEM((2 * ROWS, D), F32),
            pltpu.VMEM((CAND, QUARTER), BF),
            pltpu.VMEM((CAND, QUARTER), BF),
            pltpu.VMEM((CAND, QUARTER), BF),
            pltpu.VMEM((2 * CAND, QUARTER), BF),
            pltpu.VMEM((ROWS, 2 * CAND), BF),
            pltpu.VMEM((CAND, CAND), BF),
            pltpu.VMEM((CAND, D), BF),
            pltpu.VMEM((ROWS, D), BF),
            dma((4,)),
            dma((CHUNKS,)),
            dma((CHUNKS,)),
            dma((4 * CHUNKS,)),
            dma((8 * CHUNKS,)),
            dma((3 * CHUNKS,)),
            dma((32,)),
            dma((32,)),
            dma((64,)),
            dma((64,)),
            dma((4,)),
            dma((4,)),
            dma((2,)),
        ],
        compiler_params=pltpu.CompilerParams(
            collective_id=0, has_side_effects=True, vmem_limit_bytes=56 * 2**20
        ),
    )(
        hist_x.reshape(ROWS, D), hist_len, cand_x, cand_user.reshape(1, CAND), w_proj, w_out,
        norm_gain.reshape(1, D),
    )
    return hist_out[None], cand_out


def solution(mesh):
    in_specs = (P("cand", "seq", None), P(), P("cand", None), P("cand", None), P(), P(), P())
    out_specs = (P("cand", "seq", None), P("cand", None))
    return jax.shard_map(
        per_device, mesh=mesh, in_specs=in_specs, out_specs=out_specs, check_vma=False
    )
```

time: 484 us -> 86.4 us (0.18)
  the two profiles are of different devices: /device:TPU:1 before, /device:TPU:64 now
where the time goes in v1:
time: 86.4 us; the launch traced here: 86.2 us
  Pallas kernels  81.6 us (94%)
  local copies, waits for them, and re-layouts  3.93 us (5%)
    pallas_call x1, Pallas kernels, per_device(): pl.pallas_call(kernel, out_shape=(jax.ShapeDtypeStruct((ROWS, D), BF), ja...  81.6 us
    unnamed x2, local copies, waits for them, and re-layouts  3.93 us

profile of v1, /device:TPU:64, one launch (start us, length us, event | category | flops | bytes accessed | tf_op | source)
XLA Modules:
  0.0 86.2 jit_solution(4464205262447022242)
XLA Ops:
  0.6 81.6 %shard_map.86 = (bf16[128,1024]{1,0:T(8,128)(2,1)}, bf16[512,1024]{1,0:T(8,128)(2,1)}) custom-call(bf16[128,1024]{1,0:T(8,128)(2,1)} %bitcast.4, s32[32]{0:T(128)} %len_ref.1, bf16[512,1024]{1,0:T(8,128)(2,1)} %candx_hbm.1, s32[1,512]{1,0:T(1,128)} %bitcast.7, bf16[1024,4096]{1,0:T(8,128)(2,1)} %wp_hbm.1, bf16[1024,1024]{1,0:T(8,128)(2,1)} %wo_hbm.1, ...), custom_call_target="tpu_custom_call" | custom-call | tf_op jit(solution)/shard_map/pallas_call | solution.py:430
  82.3 1.7 %copy.11 = bf16[1,128,1024]{2,1,0:T(8,128)(2,1)} copy(bf16[1,128,1024]{2,1,0:T(8,128)(2,1)} %bitcast.5) | data formatting | bytes 524288
  83.9 2.3 %copy.12 = bf16[512,1024]{1,0:T(8,128)(2,1)} copy(bf16[512,1024]{1,0:T(8,128)(2,1)} %get-tuple-element.9) | data formatting | bytes 2097152

commit v2 on v1

v2 whole, which is shorter than its diff:
```python
import jax
import jax.numpy as jnp
from jax import lax
from jax.experimental import pallas as pl
from jax.experimental.pallas import tpu as pltpu
from jax.sharding import PartitionSpec as P


HEADS = 8
HEAD = 128
D = 1024
ROWS = 128
CHUNKS = 4
CROWS = ROWS // CHUNKS
CAND = 512
QUARTER = 256
PARTS = 2
WIDE = D // PARTS
PIECE = WIDE // 4
MESH = pl.DeviceIdType.MESH
BF = jnp.bfloat16
F32 = jnp.float32
I32 = jnp.int32
NT = (((1,), (1,)), ((), ()))


def silu(a):
    half = 0.5 * a
    return half + half * jnp.tanh(half)


def iota(shape, dim):
    return lax.broadcasted_iota(I32, shape, dim)


def onehot(condition):
    return jnp.where(condition, 1.0, 0.0).astype(BF)


def dot(a, b):
    return jnp.dot(a, b, preferred_element_type=F32)


def remote(src, dst, send, recv, seq, cand):
    return pltpu.make_async_remote_copy(
        src_ref=src, dst_ref=dst, send_sem=send, recv_sem=recv,
        device_id={"seq": seq, "cand": cand}, device_id_type=MESH,
    )


def kernel(
    x_hbm, len_ref, candx_hbm, cuser_ref, wp_hbm, wo_hbm, gain_ref,
    hist_ref, sorted_rows, unsort,
    wp, wo, candx, xb, keys, values, xc, xh, qg, acc, normed_ref, msgs, rdisp, back, rret, crep, hist_tmp,
    load_sem, swap_send, swap_recv, x_send, x_recv, fwd_send, d_send, d_recv, r_send, r_recv, g_send, g_recv, h_sem,
):
    s = lax.axis_index("seq")
    c = lax.axis_index("cand")
    x, zh = s // 2, s % 2
    core, y, zl = c % 2, (c // 2) % 4, c // 8
    z = zh * 4 + zl
    user = c - core + zh
    other_core = c + 1 - 2 * core
    early = core == zh
    late = core != zh
    swap_seq = 2 * x + core

    barrier = pltpu.get_barrier_semaphore()

    def greet(i, carry):
        pl.semaphore_signal(
            barrier, inc=1, device_id={"seq": 2 * x + (zh + i // 32) % 2, "cand": (c + i) % 32}, device_id_type=MESH
        )
        return carry

    lax.fori_loop(1, 64, greet, 0)
    for i in range(1, 4):
        pl.semaphore_signal(
            barrier, inc=1, device_id={"seq": 2 * ((x + i) % 4) + zh, "cand": c}, device_id_type=MESH
        )

    def load(src, dst, i):
        return pltpu.make_async_copy(src, dst, load_sem.at[i])

    def slot_rows(kind, there, j):
        return xb.at[pl.ds(pl.multiple_of(kind * 4 * ROWS + j * ROWS + there * CROWS, CROWS), CROWS)]

    def own_load(j):
        return load(x_hbm.at[pl.ds(j * CROWS, CROWS)], slot_rows(core, x, j), 3 + j)

    cand_load = load(candx_hbm, candx, 0)
    wp_load = load(wp_hbm, wp, 1)
    wo_load = load(wo_hbm, wo, 2)

    @pl.when(early)
    def _():
        for j in range(CHUNKS):
            own_load(j).start()

    cand_load.start()
    wp_load.start()
    wo_load.start()

    @pl.when(early)
    def _():
        for j in range(CHUNKS):
            own_load(j).wait()

    pl.semaphore_wait(barrier, 66)

    def swap_copy(j):
        return remote(
            x_hbm.at[pl.ds(j * CROWS, CROWS)], slot_rows(zh, x, j), swap_send.at[j], swap_recv.at[j], swap_seq, user
        )

    def own_copy(i, j):
        rows = slot_rows(core, x, j)
        recv = x_recv.at[(core * 4 + x) * CHUNKS + j]
        if i == 0:
            return remote(rows, rows, x_send.at[j], recv, s, other_core)
        return remote(rows, rows, x_send.at[i * CHUNKS + j], recv, 2 * ((x + i) % 4) + zh, c)

    def slot_wait(kind, there, j):
        rows = slot_rows(kind, there, j)
        recv = x_recv.at[(kind * 4 + there) * CHUNKS + j]
        remote(rows, rows, fwd_send.at[0], recv, s, other_core).wait_recv()

    def fwd_copy(i, j):
        there = (x + i) % 4
        rows = slot_rows(core, there, j)
        recv = x_recv.at[(core * 4 + there) * CHUNKS + j]
        return remote(rows, rows, fwd_send.at[(i - 1) * CHUNKS + j], recv, s, other_core)

    def send_own(j):
        for i in range(4):
            own_copy(i, j).start()

    def forward(j):
        for i in range(1, 4):
            slot_wait(core, (x + i) % 4, j)
            fwd_copy(i, j).start()

    def take(j):
        for i in range(4):
            slot_wait(1 - core, (x + i) % 4, j)

    @pl.when(late)
    def _():
        for j in range(CHUNKS):
            swap_copy(j).start()

    @pl.when(early)
    def _():
        for j in range(CHUNKS):
            send_own(j)

    owner = cuser_ref[...]
    is_user = owner == iota((32, CAND), 0)
    users = onehot(is_user)
    before = dot(users, onehot(iota((CAND, CAND), 0) < iota((CAND, CAND), 1)))
    within = jnp.sum(jnp.where(is_user, before, 0.0), axis=0, keepdims=True).astype(I32)
    smaller = dot(onehot(iota((32, 32), 1) < iota((32, 32), 0)), users)
    start = jnp.sum(smaller, axis=1, keepdims=True)
    place = jnp.sum(jnp.where(is_user, start, 0.0), axis=0, keepdims=True).astype(I32) + within
    part = place & 7
    code = owner * 32 + part * 4 + (within >> 3)
    sorted_at = ((part >> 1) << 7) + ((part & 1) << 6) + (place >> 3)

    def message(m):
        which, dy = m >> 2, m & 3
        pair = which >> 1
        dz = jnp.where(
            pair == 0, 0, jnp.where(pair == 1, 1, jnp.where(pair == 2, 7, jnp.where(which == 6, 2, 6)))
        )
        dcore = which & 1
        tz = (z + dz) & 7
        ty = (y + dy) & 3
        tcore = (core + dcore) & 1
        column = (tz & 3) * 4 + ty
        return column * 2 + (tz >> 2), tz >> 2, column * 2 + tcore, tcore

    slot = iota((CAND, 1), 0)
    to_user, _, _, to_core = message(slot >> 4)
    slot_code = to_user * 32 + (2 * x + to_core) * 4 + (slot & 3)
    match = slot_code == code
    slot_quarter = (slot >> 2) & 3
    cand_load.wait()
    sent = jnp.zeros((CAND, QUARTER), F32)
    for j in range(4):
        sent += dot(onehot(match & (slot_quarter == j)), candx[:, j * QUARTER : (j + 1) * QUARTER])
    msgs[...] = sent.astype(BF)

    def piece(ref, i):
        return ref.at[pl.ds(pl.multiple_of(i * 16, 16), 16)]

    def d_copy(m):
        _, tzh, tcand, _ = message(m)
        return remote(piece(msgs, m), piece(rdisp, c), d_send.at[m], d_recv.at[c], 2 * x + tzh, tcand)

    self_d = pltpu.make_async_copy(piece(msgs, 0), piece(rdisp, c), d_recv.at[c])
    self_d.start()

    def send_d(m, carry):
        d_copy(m).start()
        return carry

    lax.fori_loop(1, 32, send_d, 0)

    ret = iota((1024, 1), 0)
    ret_to = ret >> 4
    ret_code = (ret_to >> 1) * 32 + (2 * x + (ret_to & 1)) * 4 + (ret & 3)
    mine = iota((ROWS, 1), 0)
    mine_place = 8 * (mine & 63) + 2 * x + (mine >> 6)
    places = lax.dot_general(
        onehot(mine_place == place), onehot(ret_code == code), NT, preferred_element_type=F32
    )
    ret_quarter = (iota((ROWS, 1024), 1) >> 2) & 3
    for j in range(4):
        crep[j * ROWS : (j + 1) * ROWS, :] = jnp.where(ret_quarter == j, places, 0.0).astype(BF)
    unsort[...] = lax.dot_general(
        onehot(iota((CAND, CAND), 0) == iota((CAND, CAND), 1)),
        onehot(iota((CAND, 1), 0) == sorted_at), NT, preferred_element_type=F32,
    ).astype(BF)

    length = len_ref[user]

    def block_pos(kind, row):
        return (2 * ((row >> 5) & 3) + kind) * ROWS + (row >> 7) * CROWS + (row & (CROWS - 1))

    def project(kind, pair):
        rows = pl.ds(pl.multiple_of((kind * 2 + pair) * 2 * ROWS, 2 * ROWS), 2 * ROWS)
        alive = block_pos(kind, pair * 2 * ROWS + iota((2 * ROWS, 1), 0)) < length

        def step(n, carry):
            cols = pl.ds(pl.multiple_of(n * QUARTER, QUARTER), QUARTER)
            kcols = pl.ds(pl.multiple_of(3 * D + n * QUARTER, QUARTER), QUARTER)
            vcols = pl.ds(pl.multiple_of(D + n * QUARTER, QUARTER), QUARTER)
            keys[rows, cols] = silu(dot(xb[rows, :], wp[:, kcols])).astype(BF)
            values[rows, cols] = jnp.where(alive, silu(dot(xb[rows, :], wp[:, vcols])), 0.0).astype(BF)
            return carry

        lax.fori_loop(0, 4, step, 0, unroll=2)

    def project_q(rows_ref):
        def step(n, carry):
            cols = pl.ds(pl.multiple_of(n * QUARTER, QUARTER), QUARTER)
            qcols = pl.ds(pl.multiple_of(D + n * QUARTER, QUARTER), QUARTER)
            wcols = pl.ds(pl.multiple_of(2 * D + n * QUARTER, QUARTER), QUARTER)
            qg[:, qcols] = silu(dot(rows_ref[...], wp[:, wcols])).astype(BF)
            qg[:, cols] = silu(dot(rows_ref[...], wp[:, cols])).astype(BF)
            return carry

        lax.fori_loop(0, 4, step, 0, unroll=2)

    def attend(top, count, allowed, first):
        rows = pl.ds(top, count)
        for h in range(HEADS):
            cols = slice(h * HEAD, (h + 1) * HEAD)
            scores = lax.dot_general(
                qg[:, D + h * HEAD : D + (h + 1) * HEAD], keys[rows, cols], NT, preferred_element_type=F32
            )
            weights = silu(scores * HEAD ** -0.5)
            if allowed is not None:
                weights = jnp.where(allowed, weights, 0.0)
            mixed = dot(weights.astype(BF), values[rows, cols])
            if first:
                acc[:, cols] = mixed
            else:
                acc[:, cols] += mixed

    def kind_top(kind):
        return pl.multiple_of(kind * 4 * ROWS, 4 * ROWS)

    wp_load.wait()
    for pair in range(2):
        for j in (2 * pair, 2 * pair + 1):
            @pl.when(late)
            def _():
                swap_copy(j).wait_recv()
                send_own(j)
                take(j)

            @pl.when(early)
            def _():
                forward(j)

        project(zh, pair)

    def late_forward(j):
        @pl.when(late)
        def _():
            forward(j)

    def early_take(j):
        @pl.when(early)
        def _():
            take(j)

    late_forward(0)

    def wait_d(i, carry):
        there = (c + i) % 32
        remote(piece(rdisp, there), piece(rdisp, there), d_send.at[0], d_recv.at[there], s, other_core).wait_recv()
        return carry

    self_d.wait()
    lax.fori_loop(1, 32, wait_d, 0)
    here = iota((ROWS, CAND), 0)
    lane = iota((ROWS, CAND), 1)
    same = ((here >> 2) == (lane >> 4)) & ((here & 3) == (lane & 3))
    lane_quarter = (lane >> 2) & 3
    for j in range(4):
        xc[:, j * QUARTER : (j + 1) * QUARTER] = dot(onehot(same & (lane_quarter == j)), rdisp[...]).astype(BF)
    project_q(xc)
    late_forward(1)
    attend(kind_top(zh), 4 * ROWS, None, True)
    late_forward(2)
    early_take(0)
    early_take(1)
    project(1 - zh, 0)
    late_forward(3)
    early_take(2)
    early_take(3)
    project(1 - zh, 1)
    attend(kind_top(1 - zh), 4 * ROWS, None, False)
    wo_load.wait()

    def normalise():
        totals = acc[...]
        average = jnp.mean(totals, axis=1, keepdims=True)
        centred = totals - average
        variance = jnp.mean(centred * centred, axis=1, keepdims=True)
        normed_ref[...] = (
            centred * lax.rsqrt(variance + 1e-05) * gain_ref[...] * qg[:, 0:D].astype(F32)
        ).astype(BF)

    def finish(rows_ref, cols):
        return (dot(normed_ref[...], wo[:, cols]) + rows_ref[:, cols].astype(F32)).astype(BF)

    normalise()
    tall = iota((CAND, ROWS), 0)
    wide = iota((CAND, ROWS), 1)
    same_t = ((wide >> 2) == (tall >> 4)) & ((wide & 3) == (tall & 3))
    tall_quarter = (tall >> 2) & 3
    my_ret = user * 2 + core

    def r_copy(i, part):
        there = (c + i) % 32
        return remote(
            piece(back, part * 32 + there), piece(rret, part * 64 + my_ret), r_send.at[part * 64 + i],
            r_recv.at[part * 64 + my_ret], 2 * x + (zh + i // 32) % 2, there,
        )

    def self_r(part):
        here_r = part * 64 + my_ret
        return pltpu.make_async_copy(piece(back, part * 32 + c), piece(rret, here_r), r_recv.at[here_r])

    for part in range(PARTS):
        done = finish(xc, slice(part * WIDE, (part + 1) * WIDE))
        returned = jnp.zeros((CAND, PIECE), F32)
        for j in range(4):
            returned += dot(onehot(same_t & (tall_quarter == j)), done[:, j * PIECE : (j + 1) * PIECE])
        back[part * CAND : (part + 1) * CAND, :] = returned.astype(BF)
        self_r(part).start()

        def send_r(i, carry):
            r_copy(i, part).start()
            return carry

        lax.fori_loop(1, 64, send_r, 0)

    for j in range(CHUNKS):
        xh[j * CROWS : (j + 1) * CROWS, :] = slot_rows(core, x, j)[...]
    project_q(xh)
    query_pos = (2 * x + core) * ROWS + iota((ROWS, 1), 0)
    key = iota((1, 8 * ROWS), 1)
    attend(0, 8 * ROWS, block_pos(key >> 9, key & 511) <= query_pos, True)
    normalise()
    done_hist = finish(xh, slice(0, D))
    hist_copy = remote(hist_tmp, hist_ref, h_sem.at[0], h_sem.at[1], swap_seq, user)

    @pl.when(early)
    def _():
        hist_ref[...] = done_hist

    @pl.when(late)
    def _():
        hist_tmp[...] = done_hist

    def sorted_part(part, there):
        return sorted_rows.at[pl.ds(pl.multiple_of(part * CAND + there * ROWS, ROWS), ROWS)]

    def g_copy(i, part):
        rows = sorted_part(part, x)
        return remote(
            rows, rows, g_send.at[part * 4 + i], g_recv.at[part * 4 + x], 2 * ((x + i) % 4) + zh, c
        )

    for part in range(PARTS):
        self_r(part).wait()

        def wait_r(i, carry):
            there = part * 64 + (my_ret + i) % 64
            remote(piece(rret, there), piece(rret, there), d_send.at[0], r_recv.at[there], s, other_core).wait_recv()
            return carry

        lax.fori_loop(1, 64, wait_r, 0)
        picked = dot(crep[...], rret[part * 1024 : (part + 1) * 1024, :]).astype(BF)
        rows = pl.ds(pl.multiple_of(part * CAND + x * ROWS, ROWS), ROWS)
        for j in range(4):
            sorted_rows[rows, j * PIECE : (j + 1) * PIECE] = picked[j * ROWS : (j + 1) * ROWS, :]
        for i in range(1, 4):
            g_copy(i, part).start()

    @pl.when(late)
    def _():
        hist_copy.start()

    for part in range(PARTS):
        for i in range(1, 4):
            from_x = (x + i) % 4
            rows = sorted_part(part, from_x)
            remote(rows, rows, g_send.at[0], g_recv.at[part * 4 + from_x], s, other_core).wait_recv()

    for part in range(PARTS):
        for i in range(1, 4):
            g_copy(i, part).wait_send()

        def sent_r(i, carry):
            r_copy(i, part).wait_send()
            return carry

        lax.fori_loop(1, 64, sent_r, 0)

    def sent_d(m, carry):
        d_copy(m).wait_send()
        return carry

    lax.fori_loop(1, 32, sent_d, 0)
    for j in range(CHUNKS):
        for i in range(4):
            own_copy(i, j).wait_send()
        for i in range(1, 4):
            fwd_copy(i, j).wait_send()

    @pl.when(late)
    def _():
        for j in range(CHUNKS):
            swap_copy(j).wait_send()
        hist_copy.wait()


def last_kernel(unsort, rows_ref, hist_in, hist_ref, cand_ref):
    cand_ref[...] = dot(unsort[...], rows_ref[...]).astype(BF)
    hist_ref[...] = hist_in[...]


def per_device(hist_x, hist_len, cand_x, cand_user, w_proj, w_out, norm_gain):
    any_spec = pl.BlockSpec(memory_space=pl.ANY)
    vmem = pl.BlockSpec(memory_space=pltpu.VMEM)
    dma = pltpu.SemaphoreType.DMA
    hist_rows, sorted_rows, unsort = pl.pallas_call(
        kernel,
        out_shape=(
            jax.ShapeDtypeStruct((ROWS, D), BF),
            jax.ShapeDtypeStruct((PARTS * CAND, WIDE), BF),
            jax.ShapeDtypeStruct((CAND, CAND), BF),
        ),
        in_specs=[any_spec, pl.BlockSpec(memory_space=pltpu.SMEM), any_spec, vmem, any_spec, any_spec, vmem],
        out_specs=(vmem, vmem, vmem),
        scratch_shapes=[
            pltpu.VMEM((D, 4 * D), BF),
            pltpu.VMEM((D, D), BF),
            pltpu.VMEM((CAND, D), BF),
            pltpu.VMEM((8 * ROWS, D), BF),
            pltpu.VMEM((8 * ROWS, D), BF),
            pltpu.VMEM((8 * ROWS, D), BF),
            pltpu.VMEM((ROWS, D), BF),
            pltpu.VMEM((ROWS, D), BF),
            pltpu.VMEM((ROWS, 2 * D), BF),
            pltpu.VMEM((ROWS, D), F32),
            pltpu.VMEM((ROWS, D), BF),
            pltpu.VMEM((CAND, QUARTER), BF),
            pltpu.VMEM((CAND, QUARTER), BF),
            pltpu.VMEM((PARTS * CAND, PIECE), BF),
            pltpu.VMEM((2 * PARTS * CAND, PIECE), BF),
            pltpu.VMEM((4 * ROWS, 2 * CAND), BF),
            pltpu.VMEM((ROWS, D), BF),
            dma((3 + CHUNKS,)),
            dma((CHUNKS,)),
            dma((CHUNKS,)),
            dma((4 * CHUNKS,)),
            dma((8 * CHUNKS,)),
            dma((3 * CHUNKS,)),
            dma((32,)),
            dma((32,)),
            dma((PARTS * 64,)),
            dma((PARTS * 64,)),
            dma((PARTS * 4,)),
            dma((PARTS * 4,)),
            dma((2,)),
        ],
        compiler_params=pltpu.CompilerParams(
            collective_id=0, has_side_effects=True, vmem_limit_bytes=56 * 2**20
        ),
    )(
        hist_x.reshape(ROWS, D), hist_len, cand_x, cand_user.reshape(1, CAND), w_proj, w_out,
        norm_gain.reshape(1, D),
    )
    tiles = 4
    each = tiles // PARTS
    hist_out, cand_out = pl.pallas_call(
        last_kernel,
        grid=(tiles,),
        out_shape=(jax.ShapeDtypeStruct((ROWS, D), BF), jax.ShapeDtypeStruct((CAND, D), BF)),
        in_specs=[
            pl.BlockSpec((CAND, CAND), lambda n: (0, 0)),
            pl.BlockSpec((CAND, QUARTER), lambda n: (n // each, n % each)),
            pl.BlockSpec((ROWS, QUARTER), lambda n: (0, n)),
        ],
        out_specs=(
            pl.BlockSpec((ROWS, QUARTER), lambda n: (0, n)),
            pl.BlockSpec((CAND, QUARTER), lambda n: (0, n)),
        ),
    )(unsort, sorted_rows, hist_rows)
    return hist_out[None], cand_out


def solution(mesh):
    in_specs = (P("cand", "seq", None), P(), P("cand", None), P("cand", None), P(), P(), P())
    out_specs = (P("cand", "seq", None), P("cand", None))
    return jax.shard_map(
        per_device, mesh=mesh, in_specs=in_specs, out_specs=out_specs, check_vma=False
    )
```

time: 86.4 us -> 74.9 us (0.87)
  the two profiles are of different devices: /device:TPU:64 before, /device:TPU:1 now
where the time goes in v2:
time: 74.9 us; the launch traced here: 74.7 us
  Pallas kernels  74.1 us (99%)
    pallas_call x1, Pallas kernels, per_device(): pl.pallas_call(kernel, out_shape=(jax.ShapeDtypeStruct((ROWS, D), BF), ja...  69.9 us
    pallas_call x1, Pallas kernels, per_device(): pl.pallas_call(last_kernel, grid=(tiles,), out_shape=(jax.ShapeDtypeStruc...  4.19 us

profile of v2, /device:TPU:1, one launch (start us, length us, event | category | flops | bytes accessed | tf_op | source)
XLA Modules:
  0.0 74.7 jit_solution(13199781768958030480)
XLA Ops:
  0.6 69.9 %shard_map.86 = (bf16[128,1024]{1,0:T(8,128)(2,1)}, bf16[1024,512]{1,0:T(8,128)(2,1)}, bf16[512,512]{1,0:T(8,128)(2,1)}) custom-call(bf16[128,1024]{1,0:T(8,128)(2,1)} %bitcast.4, s32[32]{0:T(128)} %len_ref.1, bf16[512,1024]{1,0:T(8,128)(2,1)} %candx_hbm.1, s32[1,512]{1,0:T(1,128)} %bitcast.6, bf16[1024,4096]{1,0:T(8,128)(2,1)} %wp_hbm.1, ...), custom_call_target="tpu_custom_call" | custom-call | tf_op jit(solution)/shard_map/pallas_call | solution.py:462
  70.5 4.2 %shard_map.87 = (bf16[128,1024]{1,0:T(8,128)(2,1)}, bf16[512,1024]{1,0:T(8,128)(2,1)}) custom-call(bf16[512,512]{1,0:T(8,128)(2,1)} %get-tuple-element.7.unsort, bf16[1024,512]{1,0:T(8,128)(2,1)} %get-tuple-element.8.rows_ref, bf16[128,1024]{1,0:T(8,128)(2,1)} %get-tuple-element.9.hist_in), custom_call_target="tpu_custom_call" | custom-call | tf_op jit(solution)/shard_map/pallas_call | solution.py:512

commit v3 on v2

--- a/solution.py
+++ b/solution.py
@@ -50,8 +50,8 @@
 
 def kernel(
     x_hbm, len_ref, candx_hbm, cuser_ref, wp_hbm, wo_hbm, gain_ref,
-    hist_ref, sorted_rows, unsort,
-    wp, wo, candx, xb, keys, values, xc, xh, qg, acc, normed_ref, msgs, rdisp, back, rret, crep, hist_tmp,
+    hist_ref, sorted_rows, order_ref,
+    wp, wo, candx, xb, keys, values, xc, xh, qg, acc, normed_ref, msgs, rdisp, back, rret, crep, picked_rows, hist_tmp,
     load_sem, swap_send, swap_recv, x_send, x_recv, fwd_send, d_send, d_recv, r_send, r_recv, g_send, g_recv, h_sem,
 ):
     s = lax.axis_index("seq")
@@ -69,7 +69,7 @@
 
     def greet(i, carry):
         pl.semaphore_signal(
-            barrier, inc=1, device_id={"seq": 2 * x + (zh + i // 32) % 2, "cand": (c + i) % 32}, device_id_type=MESH
+            barrier, inc=1, device_id={"seq": 2 * x + ((zh + (i >> 5)) & 1), "cand": (c + i) & 31}, device_id_type=MESH
         )
         return carry
 
@@ -98,8 +98,6 @@
             own_load(j).start()
 
     cand_load.start()
-    wp_load.start()
-    wo_load.start()
 
     @pl.when(early)
     def _():
@@ -153,6 +151,9 @@
     def _():
         for j in range(CHUNKS):
             send_own(j)
+
+    wp_load.start()
+    wo_load.start()
 
     owner = cuser_ref[...]
     is_user = owner == iota((32, CAND), 0)
@@ -195,9 +196,9 @@
 
     def d_copy(m):
         _, tzh, tcand, _ = message(m)
-        return remote(piece(msgs, m), piece(rdisp, c), d_send.at[m], d_recv.at[c], 2 * x + tzh, tcand)
-
-    self_d = pltpu.make_async_copy(piece(msgs, 0), piece(rdisp, c), d_recv.at[c])
+        return remote(piece(msgs, m), piece(rdisp, c), d_send.at[0], d_recv.at[0], 2 * x + tzh, tcand)
+
+    self_d = pltpu.make_async_copy(piece(msgs, 0), piece(rdisp, c), d_recv.at[0])
     self_d.start()
 
     def send_d(m, carry):
@@ -206,30 +207,14 @@
 
     lax.fori_loop(1, 32, send_d, 0)
 
-    ret = iota((1024, 1), 0)
-    ret_to = ret >> 4
-    ret_code = (ret_to >> 1) * 32 + (2 * x + (ret_to & 1)) * 4 + (ret & 3)
-    mine = iota((ROWS, 1), 0)
-    mine_place = 8 * (mine & 63) + 2 * x + (mine >> 6)
-    places = lax.dot_general(
-        onehot(mine_place == place), onehot(ret_code == code), NT, preferred_element_type=F32
-    )
-    ret_quarter = (iota((ROWS, 1024), 1) >> 2) & 3
-    for j in range(4):
-        crep[j * ROWS : (j + 1) * ROWS, :] = jnp.where(ret_quarter == j, places, 0.0).astype(BF)
-    unsort[...] = lax.dot_general(
-        onehot(iota((CAND, CAND), 0) == iota((CAND, CAND), 1)),
-        onehot(iota((CAND, 1), 0) == sorted_at), NT, preferred_element_type=F32,
-    ).astype(BF)
-
     length = len_ref[user]
 
     def block_pos(kind, row):
         return (2 * ((row >> 5) & 3) + kind) * ROWS + (row >> 7) * CROWS + (row & (CROWS - 1))
 
-    def project(kind, pair):
-        rows = pl.ds(pl.multiple_of((kind * 2 + pair) * 2 * ROWS, 2 * ROWS), 2 * ROWS)
-        alive = block_pos(kind, pair * 2 * ROWS + iota((2 * ROWS, 1), 0)) < length
+    def project(kind, first, count):
+        rows = pl.ds(pl.multiple_of((kind * 4 + first) * ROWS, ROWS), count * ROWS)
+        alive = block_pos(kind, first * ROWS + iota((count * ROWS, 1), 0)) < length
 
         def step(n, carry):
             cols = pl.ds(pl.multiple_of(n * QUARTER, QUARTER), QUARTER)
@@ -268,23 +253,22 @@
             else:
                 acc[:, cols] += mixed
 
-    def kind_top(kind):
-        return pl.multiple_of(kind * 4 * ROWS, 4 * ROWS)
+    def pair_top(kind, pair):
+        return pl.multiple_of((kind * 2 + pair) * 2 * ROWS, 2 * ROWS)
 
     wp_load.wait()
-    for pair in range(2):
-        for j in (2 * pair, 2 * pair + 1):
-            @pl.when(late)
-            def _():
-                swap_copy(j).wait_recv()
-                send_own(j)
-                take(j)
-
-            @pl.when(early)
-            def _():
-                forward(j)
-
-        project(zh, pair)
+    for j in range(CHUNKS):
+        @pl.when(late)
+        def _():
+            swap_copy(j).wait_recv()
+            send_own(j)
+            take(j)
+
+        @pl.when(early)
+        def _():
+            forward(j)
+
+        project(zh, j, 1)
 
     def late_forward(j):
         @pl.when(late)
@@ -298,13 +282,7 @@
 
     late_forward(0)
 
-    def wait_d(i, carry):
-        there = (c + i) % 32
-        remote(piece(rdisp, there), piece(rdisp, there), d_send.at[0], d_recv.at[there], s, other_core).wait_recv()
-        return carry
-
-    self_d.wait()
-    lax.fori_loop(1, 32, wait_d, 0)
+    pltpu.make_async_copy(rdisp, rdisp, d_recv.at[0]).wait()
     here = iota((ROWS, CAND), 0)
     lane = iota((ROWS, CAND), 1)
     same = ((here >> 2) == (lane >> 4)) & ((here & 3) == (lane & 3))
@@ -313,16 +291,17 @@
         xc[:, j * QUARTER : (j + 1) * QUARTER] = dot(onehot(same & (lane_quarter == j)), rdisp[...]).astype(BF)
     project_q(xc)
     late_forward(1)
-    attend(kind_top(zh), 4 * ROWS, None, True)
+    attend(pair_top(zh, 0), 4 * ROWS, None, True)
     late_forward(2)
+    late_forward(3)
     early_take(0)
     early_take(1)
-    project(1 - zh, 0)
-    late_forward(3)
+    project(1 - zh, 0, 2)
+    attend(pair_top(1 - zh, 0), 2 * ROWS, None, False)
     early_take(2)
     early_take(3)
-    project(1 - zh, 1)
-    attend(kind_top(1 - zh), 4 * ROWS, None, False)
+    project(1 - zh, 2, 2)
+    attend(pair_top(1 - zh, 1), 2 * ROWS, None, False)
     wo_load.wait()
 
     def normalise():
@@ -345,15 +324,16 @@
     my_ret = user * 2 + core
 
     def r_copy(i, part):
-        there = (c + i) % 32
+        there = (c + i) & 31
         return remote(
-            piece(back, part * 32 + there), piece(rret, part * 64 + my_ret), r_send.at[part * 64 + i],
-            r_recv.at[part * 64 + my_ret], 2 * x + (zh + i // 32) % 2, there,
+            piece(back, part * 32 + there), piece(rret, part * 64 + my_ret), r_send.at[part],
+            r_recv.at[part], 2 * x + ((zh + (i >> 5)) & 1), there,
         )
 
     def self_r(part):
-        here_r = part * 64 + my_ret
-        return pltpu.make_async_copy(piece(back, part * 32 + c), piece(rret, here_r), r_recv.at[here_r])
+        return pltpu.make_async_copy(
+            piece(back, part * 32 + c), piece(rret, part * 64 + my_ret), r_recv.at[part]
+        )
 
     for part in range(PARTS):
         done = finish(xc, slice(part * WIDE, (part + 1) * WIDE))
@@ -367,7 +347,20 @@
             r_copy(i, part).start()
             return carry
 
-        lax.fori_loop(1, 64, send_r, 0)
+        lax.fori_loop(1, 64, send_r, 0, unroll=7)
+
+    ret = iota((1024, 1), 0)
+    ret_to = ret >> 4
+    ret_code = (ret_to >> 1) * 32 + (2 * x + (ret_to & 1)) * 4 + (ret & 3)
+    mine = iota((ROWS, 1), 0)
+    mine_place = 8 * (mine & 63) + 2 * x + (mine >> 6)
+    places = lax.dot_general(
+        onehot(mine_place == place), onehot(ret_code == code), NT, preferred_element_type=F32
+    )
+    ret_quarter = (iota((ROWS, 1024), 1) >> 2) & 3
+    for j in range(4):
+        crep[j * ROWS : (j + 1) * ROWS, :] = jnp.where(ret_quarter == j, places, 0.0).astype(BF)
+    order_ref[...] = sorted_at
 
     for j in range(CHUNKS):
         xh[j * CROWS : (j + 1) * CROWS, :] = slot_rows(core, x, j)[...]
@@ -376,41 +369,40 @@
     key = iota((1, 8 * ROWS), 1)
     attend(0, 8 * ROWS, block_pos(key >> 9, key & 511) <= query_pos, True)
     normalise()
-    done_hist = finish(xh, slice(0, D))
+    hist_tmp[...] = finish(xh, slice(0, D))
     hist_copy = remote(hist_tmp, hist_ref, h_sem.at[0], h_sem.at[1], swap_seq, user)
 
+    hist_home = pltpu.make_async_copy(hist_tmp, hist_ref, h_sem.at[0])
+
     @pl.when(early)
     def _():
-        hist_ref[...] = done_hist
-
-    @pl.when(late)
-    def _():
-        hist_tmp[...] = done_hist
+        hist_home.start()
 
     def sorted_part(part, there):
         return sorted_rows.at[pl.ds(pl.multiple_of(part * CAND + there * ROWS, ROWS), ROWS)]
 
+    def picked_part(part):
+        return picked_rows.at[part * ROWS : (part + 1) * ROWS]
+
+    def g_home(part):
+        return pltpu.make_async_copy(picked_part(part), sorted_part(part, x), g_send.at[part * 4])
+
     def g_copy(i, part):
-        rows = sorted_part(part, x)
         return remote(
-            rows, rows, g_send.at[part * 4 + i], g_recv.at[part * 4 + x], 2 * ((x + i) % 4) + zh, c
+            picked_part(part), sorted_part(part, x), g_send.at[part * 4 + i], g_recv.at[part * 4 + x], 2 * ((x + i) % 4) + zh, c
         )
 
     for part in range(PARTS):
-        self_r(part).wait()
-
-        def wait_r(i, carry):
-            there = part * 64 + (my_ret + i) % 64
-            remote(piece(rret, there), piece(rret, there), d_send.at[0], r_recv.at[there], s, other_core).wait_recv()
-            return carry
-
-        lax.fori_loop(1, 64, wait_r, 0)
+        arrived = rret.at[part * 1024 : (part + 1) * 1024]
+        pltpu.make_async_copy(arrived, arrived, r_recv.at[part]).wait()
         picked = dot(crep[...], rret[part * 1024 : (part + 1) * 1024, :]).astype(BF)
-        rows = pl.ds(pl.multiple_of(part * CAND + x * ROWS, ROWS), ROWS)
         for j in range(4):
-            sorted_rows[rows, j * PIECE : (j + 1) * PIECE] = picked[j * ROWS : (j + 1) * ROWS, :]
+            picked_rows[part * ROWS : (part + 1) * ROWS, j * PIECE : (j + 1) * PIECE] = picked[
+                j * ROWS : (j + 1) * ROWS, :
+            ]
         for i in range(1, 4):
             g_copy(i, part).start()
+        g_home(part).start()
 
     @pl.when(late)
     def _():
@@ -425,18 +417,13 @@
     for part in range(PARTS):
         for i in range(1, 4):
             g_copy(i, part).wait_send()
-
-        def sent_r(i, carry):
-            r_copy(i, part).wait_send()
-            return carry
-
-        lax.fori_loop(1, 64, sent_r, 0)
-
-    def sent_d(m, carry):
-        d_copy(m).wait_send()
-        return carry
-
-    lax.fori_loop(1, 32, sent_d, 0)
+        g_home(part).wait()
+
+        gone = rret.at[pl.ds(part * 1024, 63 * 16)]
+        remote(gone, gone, r_send.at[part], r_recv.at[part], s, other_core).wait_send()
+
+    left = rdisp.at[pl.ds(0, 31 * 16)]
+    remote(left, left, d_send.at[0], d_recv.at[0], s, other_core).wait_send()
     for j in range(CHUNKS):
         for i in range(4):
             own_copy(i, j).wait_send()
@@ -449,25 +436,52 @@
             swap_copy(j).wait_send()
         hist_copy.wait()
 
-
-def last_kernel(unsort, rows_ref, hist_in, hist_ref, cand_ref):
-    cand_ref[...] = dot(unsort[...], rows_ref[...]).astype(BF)
-    hist_ref[...] = hist_in[...]
+    @pl.when(early)
+    def _():
+        hist_home.wait()
+
+
+def last_kernel(order_ref, rows_hbm, hist_hbm, hist_ref, cand_ref, rows, out, hist, load_sem, store_sem):
+    hist_load = pltpu.make_async_copy(hist_hbm, hist, load_sem.at[4])
+    hist_load.start()
+    loads, stores = [], []
+    for n in range(4):
+        part, first = n * QUARTER // WIDE, n * QUARTER % WIDE
+        src = rows_hbm.at[pl.ds(part * CAND, CAND), pl.ds(first, QUARTER)]
+        loads.append(pltpu.make_async_copy(src, rows.at[n], load_sem.at[n]))
+        loads[n].start()
+    unsort = lax.dot_general(
+        onehot(iota((CAND, CAND), 0) == iota((CAND, CAND), 1)),
+        onehot(iota((CAND, 1), 0) == order_ref[...]), NT, preferred_element_type=F32,
+    ).astype(BF)
+    for n in range(4):
+        loads[n].wait()
+        out[n] = dot(unsort, rows[n]).astype(BF)
+        stores.append(
+            pltpu.make_async_copy(out.at[n], cand_ref.at[:, pl.ds(n * QUARTER, QUARTER)], store_sem.at[n])
+        )
+        stores[-1].start()
+        if n == 0:
+            hist_load.wait()
+            stores.append(pltpu.make_async_copy(hist, hist_ref, store_sem.at[4]))
+            stores[1].start()
+    for store in stores:
+        store.wait()
 
 
 def per_device(hist_x, hist_len, cand_x, cand_user, w_proj, w_out, norm_gain):
     any_spec = pl.BlockSpec(memory_space=pl.ANY)
     vmem = pl.BlockSpec(memory_space=pltpu.VMEM)
     dma = pltpu.SemaphoreType.DMA
-    hist_rows, sorted_rows, unsort = pl.pallas_call(
+    hist_rows, sorted_rows, order = pl.pallas_call(
         kernel,
         out_shape=(
             jax.ShapeDtypeStruct((ROWS, D), BF),
             jax.ShapeDtypeStruct((PARTS * CAND, WIDE), BF),
-            jax.ShapeDtypeStruct((CAND, CAND), BF),
+            jax.ShapeDtypeStruct((1, CAND), I32),
         ),
         in_specs=[any_spec, pl.BlockSpec(memory_space=pltpu.SMEM), any_spec, vmem, any_spec, any_spec, vmem],
-        out_specs=(vmem, vmem, vmem),
+        out_specs=(any_spec, any_spec, vmem),
         scratch_shapes=[
             pltpu.VMEM((D, 4 * D), BF),
             pltpu.VMEM((D, D), BF),
@@ -485,6 +499,7 @@
             pltpu.VMEM((PARTS * CAND, PIECE), BF),
             pltpu.VMEM((2 * PARTS * CAND, PIECE), BF),
             pltpu.VMEM((4 * ROWS, 2 * CAND), BF),
+            pltpu.VMEM((PARTS * ROWS, WIDE), BF),
             pltpu.VMEM((ROWS, D), BF),
             dma((3 + CHUNKS,)),
             dma((CHUNKS,)),
@@ -492,10 +507,10 @@
             dma((4 * CHUNKS,)),
             dma((8 * CHUNKS,)),
             dma((3 * CHUNKS,)),
-            dma((32,)),
-            dma((32,)),
-            dma((PARTS * 64,)),
-            dma((PARTS * 64,)),
+            dma((1,)),
+            dma((1,)),
+            dma((PARTS,)),
+            dma((PARTS,)),
             dma((PARTS * 4,)),
             dma((PARTS * 4,)),
             dma((2,)),
@@ -507,22 +522,20 @@
         hist_x.reshape(ROWS, D), hist_len, cand_x, cand_user.reshape(1, CAND), w_proj, w_out,
         norm_gain.reshape(1, D),
     )
-    tiles = 4
-    each = tiles // PARTS
     hist_out, cand_out = pl.pallas_call(
         last_kernel,
-        grid=(tiles,),
         out_shape=(jax.ShapeDtypeStruct((ROWS, D), BF), jax.ShapeDtypeStruct((CAND, D), BF)),
-        in_specs=[
-            pl.BlockSpec((CAND, CAND), lambda n: (0, 0)),
-            pl.BlockSpec((CAND, QUARTER), lambda n: (n // each, n % each)),
-            pl.BlockSpec((ROWS, QUARTER), lambda n: (0, n)),
+        in_specs=[vmem, any_spec, any_spec],
+        out_specs=(any_spec, any_spec),
+        scratch_shapes=[
+            pltpu.VMEM((4, CAND, QUARTER), BF),
+            pltpu.VMEM((4, CAND, QUARTER), BF),
+            pltpu.VMEM((ROWS, D), BF),
+            dma((5,)),
+            dma((5,)),
         ],
-        out_specs=(
-            pl.BlockSpec((ROWS, QUARTER), lambda n: (0, n)),
-            pl.BlockSpec((CAND, QUARTER), lambda n: (0, n)),
-        ),
-    )(unsort, sorted_rows, hist_rows)
+        compiler_params=pltpu.CompilerParams(vmem_limit_bytes=56 * 2**20),
+    )(order, sorted_rows, hist_rows)
     return hist_out[None], cand_out
 
 

time: 74.9 us -> 68.9 us (0.920)
  Pallas kernels: 74.1 us -> 67.9 us
    pallas_call x1, Pallas kernels: 69.9 us -> 63.7 us  [per_device(): pl.pallas_call(kernel, out_shape=(jax.ShapeDtypeStruct((ROWS, D), BF), ja...]
where the time goes in v3:
time: 68.9 us; the launch traced here: 68.7 us
  Pallas kernels  67.9 us (99%)
  between operations  0.8 us (1%)
    pallas_call x1, Pallas kernels, per_device(): pl.pallas_call(kernel, out_shape=(jax.ShapeDtypeStruct((ROWS, D), BF), ja...  63.7 us
    pallas_call x1, Pallas kernels, per_device(): pl.pallas_call(last_kernel, out_shape=(jax.ShapeDtypeStruct((ROWS, D), BF...  4.18 us

profile of v3, /device:TPU:1, one launch (start us, length us, event | category | flops | bytes accessed | tf_op | source)
XLA Modules:
  0.0 68.7 jit_solution(9960183089941571585)
XLA Ops:
  0.6 63.7 %shard_map.86 = (bf16[128,1024]{1,0:T(8,128)(2,1)}, bf16[1024,512]{1,0:T(8,128)(2,1)}, s32[1,512]{1,0:T(1,128)}) custom-call(bf16[128,1024]{1,0:T(8,128)(2,1)} %bitcast.4, s32[32]{0:T(128)} %len_ref.1, bf16[512,1024]{1,0:T(8,128)(2,1)} %candx_hbm.1, s32[1,512]{1,0:T(1,128)} %bitcast.6, bf16[1024,4096]{1,0:T(8,128)(2,1)} %wp_hbm.1, ...), custom_call_target="tpu_custom_call" | custom-call | tf_op jit(solution)/shard_map/pallas_call | solution.py:476
  64.4 4.2 %shard_map.87 = (bf16[128,1024]{1,0:T(8,128)(2,1)}, bf16[512,1024]{1,0:T(8,128)(2,1)}) custom-call(s32[1,512]{1,0:T(1,128)} %get-tuple-element.7.order_ref, bf16[1024,512]{1,0:T(8,128)(2,1)} %get-tuple-element.8.rows_hbm, bf16[128,1024]{1,0:T(8,128)(2,1)} %get-tuple-element.9.hist_hbm), custom_call_target="tpu_custom_call" | custom-call | tf_op jit(solution)/shard_map/pallas_call | solution.py:525

commit v4 on v3

--- a/solution.py
+++ b/solution.py
@@ -445,20 +445,19 @@
     hist_load = pltpu.make_async_copy(hist_hbm, hist, load_sem.at[4])
     hist_load.start()
     loads, stores = [], []
-    for n in range(4):
-        part, first = n * QUARTER // WIDE, n * QUARTER % WIDE
-        src = rows_hbm.at[pl.ds(part * CAND, CAND), pl.ds(first, QUARTER)]
+    for n in range(PARTS):
+        src = rows_hbm.at[pl.ds(n * CAND, CAND)]
         loads.append(pltpu.make_async_copy(src, rows.at[n], load_sem.at[n]))
         loads[n].start()
     unsort = lax.dot_general(
         onehot(iota((CAND, CAND), 0) == iota((CAND, CAND), 1)),
         onehot(iota((CAND, 1), 0) == order_ref[...]), NT, preferred_element_type=F32,
     ).astype(BF)
-    for n in range(4):
+    for n in range(PARTS):
         loads[n].wait()
         out[n] = dot(unsort, rows[n]).astype(BF)
         stores.append(
-            pltpu.make_async_copy(out.at[n], cand_ref.at[:, pl.ds(n * QUARTER, QUARTER)], store_sem.at[n])
+            pltpu.make_async_copy(out.at[n], cand_ref.at[:, pl.ds(n * WIDE, WIDE)], store_sem.at[n])
         )
         stores[-1].start()
         if n == 0:
@@ -528,8 +527,8 @@
         in_specs=[vmem, any_spec, any_spec],
         out_specs=(any_spec, any_spec),
         scratch_shapes=[
-            pltpu.VMEM((4, CAND, QUARTER), BF),
-            pltpu.VMEM((4, CAND, QUARTER), BF),
+            pltpu.VMEM((PARTS, CAND, WIDE), BF),
+            pltpu.VMEM((PARTS, CAND, WIDE), BF),
             pltpu.VMEM((ROWS, D), BF),
             dma((5,)),
             dma((5,)),

time: 68.9 us -> 68.3 us (level)
  no operation moved by 1% of the time
where the time goes in v4:
time: 68.3 us; the launch traced here: 68.1 us
  Pallas kernels  67.3 us (99%)
  between operations  0.8 us (1%)
    pallas_call x1, Pallas kernels, per_device(): pl.pallas_call(kernel, out_shape=(jax.ShapeDtypeStruct((ROWS, D), BF), ja...  63.7 us
    pallas_call x1, Pallas kernels, per_device(): pl.pallas_call(last_kernel, out_shape=(jax.ShapeDtypeStruct((ROWS, D), BF...  3.56 us

profile of v4, /device:TPU:1, one launch (start us, length us, event | category | flops | bytes accessed | tf_op | source)
XLA Modules:
  0.0 68.1 jit_solution(7015781305367063558)
XLA Ops:
  0.6 63.7 %shard_map.86 = (bf16[128,1024]{1,0:T(8,128)(2,1)}, bf16[1024,512]{1,0:T(8,128)(2,1)}, s32[1,512]{1,0:T(1,128)}) custom-call(bf16[128,1024]{1,0:T(8,128)(2,1)} %bitcast.4, s32[32]{0:T(128)} %len_ref.1, bf16[512,1024]{1,0:T(8,128)(2,1)} %candx_hbm.1, s32[1,512]{1,0:T(1,128)} %bitcast.6, bf16[1024,4096]{1,0:T(8,128)(2,1)} %wp_hbm.1, ...), custom_call_target="tpu_custom_call" | custom-call | tf_op jit(solution)/shard_map/pallas_call | solution.py:475
  64.4 3.6 %shard_map.87 = (bf16[128,1024]{1,0:T(8,128)(2,1)}, bf16[512,1024]{1,0:T(8,128)(2,1)}) custom-call(s32[1,512]{1,0:T(1,128)} %get-tuple-element.7.order_ref, bf16[1024,512]{1,0:T(8,128)(2,1)} %get-tuple-element.8.rows_hbm, bf16[128,1024]{1,0:T(8,128)(2,1)} %get-tuple-element.9.hist_hbm), custom_call_target="tpu_custom_call" | custom-call | tf_op jit(solution)/shard_map/pallas_call | solution.py:524

commit v5 on v4

--- a/solution.py
+++ b/solution.py
@@ -224,7 +224,7 @@
             values[rows, cols] = jnp.where(alive, silu(dot(xb[rows, :], wp[:, vcols])), 0.0).astype(BF)
             return carry
 
-        lax.fori_loop(0, 4, step, 0, unroll=2)
+        lax.fori_loop(0, 4, step, 0, unroll=4)
 
     def project_q(rows_ref):
         def step(n, carry):
@@ -235,7 +235,7 @@
             qg[:, cols] = silu(dot(rows_ref[...], wp[:, cols])).astype(BF)
             return carry
 
-        lax.fori_loop(0, 4, step, 0, unroll=2)
+        lax.fori_loop(0, 4, step, 0, unroll=4)
 
     def attend(top, count, allowed, first):
         rows = pl.ds(top, count)

time: 68.3 us -> 64.7 us (0.947)
  Pallas kernels: 67.3 us -> 63.7 us
    pallas_call x1, Pallas kernels: 63.7 us -> 60.1 us  [per_device(): pl.pallas_call(kernel, out_shape=(jax.ShapeDtypeStruct((ROWS, D), BF), ja...]
where the time goes in v5:
time: 64.7 us; the launch traced here: 64.5 us
  Pallas kernels  63.7 us (98%)
  between operations  0.8 us (1%)
    pallas_call x1, Pallas kernels, per_device(): pl.pallas_call(kernel, out_shape=(jax.ShapeDtypeStruct((ROWS, D), BF), ja...  60.1 us
    pallas_call x1, Pallas kernels, per_device(): pl.pallas_call(last_kernel, out_shape=(jax.ShapeDtypeStruct((ROWS, D), BF...  3.56 us

profile of v5, /device:TPU:1, one launch (start us, length us, event | category | flops | bytes accessed | tf_op | source)
XLA Modules:
  0.0 64.5 jit_solution(11951923584718820367)
XLA Ops:
  0.6 60.1 %shard_map.86 = (bf16[128,1024]{1,0:T(8,128)(2,1)}, bf16[1024,512]{1,0:T(8,128)(2,1)}, s32[1,512]{1,0:T(1,128)}) custom-call(bf16[128,1024]{1,0:T(8,128)(2,1)} %bitcast.4, s32[32]{0:T(128)} %len_ref.1, bf16[512,1024]{1,0:T(8,128)(2,1)} %candx_hbm.1, s32[1,512]{1,0:T(1,128)} %bitcast.6, bf16[1024,4096]{1,0:T(8,128)(2,1)} %wp_hbm.1, ...), custom_call_target="tpu_custom_call" | custom-call | tf_op jit(solution)/shard_map/pallas_call | solution.py:475
  60.8 3.6 %shard_map.87 = (bf16[128,1024]{1,0:T(8,128)(2,1)}, bf16[512,1024]{1,0:T(8,128)(2,1)}) custom-call(s32[1,512]{1,0:T(1,128)} %get-tuple-element.7.order_ref, bf16[1024,512]{1,0:T(8,128)(2,1)} %get-tuple-element.8.rows_hbm, bf16[128,1024]{1,0:T(8,128)(2,1)} %get-tuple-element.9.hist_hbm), custom_call_target="tpu_custom_call" | custom-call | tf_op jit(solution)/shard_map/pallas_call | solution.py:524
